TPU v7x, 32 devices: a whole 2x2x4 slice. The times are simulated.
32 devices in a mesh: rows: 8 (over z, x), feat: 4 (over y, core).
Axes of the slice: x: 2, y: 2, z: 4, core: 2. Of those that a mesh axis runs over, the one named last changes fastest.
Arguments:
- scores: float32 [262144, 64], P(('rows', 'feat'))
- labels: int32 [262144], P('rows'), may hold values from 0 to 63
- bins: int32 [256, 262144], P('feat', 'rows'), may hold values from 0 to 63
- elected: int32 [64, 16], P(None, 'feat'), may hold values from 0 to 255, as said below
Outputs:
- gains: float32 [64, 16, 63], P('rows', 'feat')
Inputs may be any that keep to these rules, and one draw needn't show every extreme that they name: `elected`: for every class and every j < 4, columns j * 4 to (j + 1) * 4 - 1 hold 4 distinct features of the range j * 64 to (j + 1) * 64 - 1.
All inputs are finite; a program needn't handle non-finite values.
Results may differ from a plain program's by a relative error of at most 0.0026.
Values may be sent and summed in bfloat16 or wider, within the bound.
No kernel may reach another device: no remote copies, remote signals or barrier semaphores. Data moves between devices by JAX's collectives and lax.ppermute only.
A program may use at most 64 MiB of HBM per device.

v0:
```python
import jax
import jax.numpy as jnp
from jax import lax
from jax.experimental import pallas as pl
from jax.experimental.pallas import tpu as pltpu
from jax.sharding import PartitionSpec as P

BINS = 64
l2_penalty = 1.0

SURE = -1e-30

F8 = jnp.float8_e4m3fn
FULL = 256.0
LOW = 16.0


def rounded(x):
    far = x * 65537.0
    return far - (far - x)


def nudged(code, side, wanted):
    code = rounded(code)
    found = rounded(code + side)
    unit = jnp.abs(code) * (1.25 / 256.0)
    return jnp.where(wanted > found, code + unit, jnp.where(wanted < found, code - unit, code))


def score_kernel(n_blocks, scores_ref, labels_ref, coded_ref, score_slots, label_slot, sems):
    rows = scores_ref.shape[1]
    block = rows // n_blocks
    begin = pl.multiple_of(lax.axis_index("feat") * rows, rows)
    label_copy = pltpu.make_async_copy(labels_ref.at[:, pl.ds(begin, rows)], label_slot, sems.at[n_blocks])
    label_copy.start()
    copies = [
        pltpu.make_async_copy(
            scores_ref.at[:, pl.ds(i * block, block)], score_slots.at[:, pl.ds(i * block, block)], sems.at[i]
        )
        for i in range(n_blocks)
    ]
    for copy in copies:
        copy.start()
    label_copy.wait()
    for i in range(n_blocks):
        copies[i].wait()
        where = pl.ds(i * block, block)
        coded_ref[:, where] = encode(score_slots[:, where], label_slot[:, where]).astype(coded_ref.dtype)


def encode(scores, labels):
    is_label = lax.broadcasted_iota(jnp.int32, scores.shape, 0) == labels
    row_max = jnp.max(scores, axis=0, keepdims=True)
    expon = jnp.exp(scores - row_max)
    top = 1.0 / jnp.sum(expon, axis=0, keepdims=True)
    probs = expon * top
    labelled = jnp.sum(jnp.where(is_label, probs, 0.0), axis=0, keepdims=True)
    top_code = nudged(jnp.minimum(top - 1.0, SURE), 1.0, rounded(top))
    label_code = jnp.where(
        labelled > 0.5,
        jnp.minimum(labelled - 1.0, SURE),
        nudged(labelled, -1.0, rounded(labelled - 1.0)),
    )
    return jnp.where(is_label, label_code, jnp.where(probs > 0.5, top_code, probs))


def in_hbm(array):
    return pltpu.with_memory_space_constraint(array, pltpu.HBM)


def score(scores, labels):
    classes, rows = scores.shape
    n_blocks = 4
    far = pl.BlockSpec(memory_space=pltpu.HBM)
    return pl.pallas_call(
        lambda *refs: score_kernel(n_blocks, *refs),
        in_specs=[far, far],
        out_specs=pl.BlockSpec(memory_space=pltpu.VMEM),
        scratch_shapes=[
            pltpu.VMEM((classes, rows), jnp.float32),
            pltpu.VMEM((1, rows), jnp.int32),
            pltpu.SemaphoreType.DMA((n_blocks + 1,)),
        ],
        out_shape=jax.ShapeDtypeStruct((classes, rows), jnp.bfloat16),
        compiler_params=pltpu.CompilerParams(vmem_limit_bytes=36 << 20),
        cost_estimate=pl.CostEstimate(
            flops=10 * rows * classes, bytes_accessed=6 * rows * classes, transcendentals=rows * classes
        ),
    )(in_hbm(scores), in_hbm(labels))


def decode(coded, labels):
    classes, length = coded.shape
    kind = coded.dtype
    class_ids = lax.broadcasted_iota(jnp.int32, (classes, length), 0).astype(kind)
    is_label = class_ids == labels.astype(kind)
    zero, one = jnp.zeros_like(coded), jnp.ones_like(coded)
    above = coded < zero
    side = jnp.where(above, one, -one)
    crossed = is_label != above
    near = jnp.where(crossed, (coded + side) - side, coded)
    whole = jnp.where(crossed, side, zero)
    return near, whole, (near - jnp.abs(coded)) + coded * coded


def scales(coded):
    largest = jnp.max(jnp.abs(coded), axis=1, keepdims=True).astype(jnp.float32)
    scale = jnp.ones_like(largest)
    back = jnp.ones_like(largest)
    for power in (16, 8, 4, 2, 1):
        small = largest * scale <= 0.5**power
        scale = jnp.where(small, scale * 2.0**power, scale)
        back = jnp.where(small, back * 0.5**power, back)
    return (scale * (FULL / 2)).astype(coded.dtype), back * (2 / FULL)


def put_backs(coded_ref, backs_ref, scales_ref):
    classes = coded_ref.shape[0]
    scale, back = scales(coded_ref[...])
    scales_ref[...] = jnp.broadcast_to(scale, scales_ref.shape)
    for kind, factor in enumerate((back, back * (1.0 / LOW), back, jnp.ones_like(back))):
        backs_ref[kind * classes : (kind + 1) * classes, :] = jnp.broadcast_to(
            factor, (classes, backs_ref.shape[1])
        )


def put_columns(coded_ref, labels_ref, begin, length, columns_ref, scales_ref):
    classes = coded_ref.shape[0]
    rows = pl.ds(begin, length)
    scale = scales_ref[:, :1]
    near, whole, square = decode(coded_ref[:, rows], labels_ref[:, rows])
    scaled = near * scale
    high = scaled.astype(F8)
    low = ((scaled - high.astype(scaled.dtype)) * LOW).astype(F8)
    for kind, part in enumerate((high, low, (square * scale).astype(F8), whole.astype(F8))):
        columns_ref[kind * classes : (kind + 1) * classes, rows] = part


def back_row(backs_ref):
    rows, lanes = backs_ref.shape
    sub = lax.broadcasted_iota(jnp.int32, (lanes, lanes), 0)
    diagonal = sub == lax.broadcasted_iota(jnp.int32, (lanes, lanes), 1)
    parts = [
        jnp.sum(jnp.where(diagonal, backs_ref[start : start + lanes, :], 0.0), axis=0, keepdims=True)
        for start in range(0, rows, lanes)
    ]
    return jnp.concatenate(parts, axis=1)


def add_tile(bins_ref, columns_ref, back, sums_ref, first_feature, count, fresh):
    length = bins_ref.shape[1]
    rows = BINS // 2
    bin_ids = lax.broadcasted_iota(jnp.int32, (rows, length), 0)
    low_ids, high_ids = bin_ids.astype(jnp.int8), (bin_ids + rows).astype(jnp.int8)
    one = jnp.ones((rows, length), F8)
    zero = jnp.zeros((rows, length), F8)
    parts = []
    for offset in range(count):
        codes = jnp.broadcast_to(bins_ref[pl.ds(first_feature + offset, 1), :], (rows, length))
        codes = codes.astype(jnp.int8)
        parts.append(jnp.where(codes == low_ids, one, zero))
        parts.append(jnp.where(codes == high_ids, one, zero))
    added = lax.dot_general(
        jnp.concatenate(parts, axis=0),
        columns_ref[...],
        (((1,), (1,)), ((), ())),
        preferred_element_type=jnp.float32,
    )
    added = added * back
    where = pl.ds(pl.multiple_of(first_feature * BINS, count * BINS), count * BINS)
    if fresh:
        sums_ref[where, :] = added
    else:
        sums_ref[where, :] += added


def hist_kernel(group, length, shifts, n_feat, cores, chained, final, *refs):
    count = len(shifts)
    elect_ref, bins_ref, labels_ref = refs[:3]
    coded_refs = refs[3 : 3 + count]
    refs = refs[3 + count :]
    refs = refs[1:] if chained else refs
    sums_ref, refs = refs[0], refs[1:]
    if final:
        out_ref, refs = refs[0], refs[1:]
    bin_slots, label_slots, coded_slots = refs[:3]
    columns = refs[3:5]
    backs = refs[5:7]
    bin_sems, label_sems, coded_sems, elect_slot, elect_sem, scales_ref = refs[7:]
    classes, rows = coded_refs[0].shape
    features = bins_ref.shape[0]
    place = lax.axis_index("feat")
    halves = rows // length
    blocks = [(part, half) for part in range(count) for half in range(halves)]

    bin_copies, code_copies = [], []
    for index, (part, half) in enumerate(blocks):
        turn, swapped = shifts[part]
        source = (place - turn * cores + n_feat) % n_feat
        if swapped:
            source = source + 1 - 2 * (source % 2)
        begin = pl.multiple_of(source * rows + half * length, length)
        bin_copies.append(
            pltpu.make_async_copy(
                bins_ref.at[:, pl.ds(begin, length)], bin_slots.at[index % 2], bin_sems.at[index]
            )
        )
        code_copies.append(
            (
                pltpu.make_async_copy(
                    coded_refs[part].at[:, pl.ds(half * length, length)],
                    coded_slots.at[index],
                    coded_sems.at[index],
                ),
                pltpu.make_async_copy(
                    labels_ref.at[:, pl.ds(begin, length)], label_slots.at[index], label_sems.at[index]
                ),
            )
        )
    if final:
        elect_copy = pltpu.make_async_copy(elect_ref, elect_slot, elect_sem)
        elect_copy.start()
    for copy in code_copies[0]:
        copy.start()
    bin_copies[0].start()
    bin_copies[1].start()
    for pair in code_copies[1:]:
        for copy in pair:
            copy.start()

    tiles = features // group
    turns = 2 if len(blocks) > 2 and tiles % 2 == 0 else 1
    chunk = length // tiles
    for copy in code_copies[0]:
        copy.wait()
    put_backs(coded_slots.at[0], backs[0], scales_ref)
    put_columns(coded_slots.at[0], label_slots.at[0], 0, length, columns[0], scales_ref)

    for index in range(len(blocks)):
        now, later = index % 2, (index + 1) % 2
        back = back_row(backs[now])
        bin_copies[index].wait()
        more = index + 1 < len(blocks)
        fresh = index == 0 and not chained
        if more:
            for copy in code_copies[index + 1]:
                copy.wait()

        if more:
            put_backs(coded_slots.at[index + 1], backs[later], scales_ref)

        def one_turn(turn, carry):
            for offset in range(tiles // turns):
                tile = turn * (tiles // turns) + offset
                add_tile(bin_slots.at[now], columns[now], back, sums_ref, tile * group, group, fresh)
                if more:
                    put_columns(
                        coded_slots.at[index + 1],
                        label_slots.at[index + 1],
                        pl.multiple_of(tile * chunk, chunk),
                        chunk,
                        columns[later],
                        scales_ref,
                    )
            return carry

        if turns == 1:
            one_turn(0, 0)
        else:
            lax.fori_loop(0, turns, one_turn, 0)
        if index + 2 < len(blocks):
            bin_copies[index + 2].start()

    if not final:
        return
    elect_copy.wait()
    width = 2 * classes
    elected = jnp.concatenate([elect_slot[...]] * 2, axis=1) - place * features
    elect = elected.shape[0]
    by_class = []
    for half in range(2):

        def pick(feature, picked):
            rows = sums_ref[
                pl.ds(pl.multiple_of(feature * BINS, BINS), BINS), half * width : (half + 1) * width
            ]
            return tuple(jnp.where(elected[e : e + 1, :] == feature, rows, picked[e]) for e in range(elect))

        nothing = tuple(jnp.zeros((BINS, width), jnp.float32) for _ in range(elect))
        picked = lax.fori_loop(0, features, pick, nothing, unroll=2)
        by_class.append(jnp.concatenate([part.T for part in picked], axis=1))
    near = by_class[0][:classes] + by_class[0][classes:]
    square, whole = by_class[1][:classes], by_class[1][classes:]
    kinds = (near + whole, near - square)
    owners, _, owned, _ = out_ref.shape
    for owner in range(owners):
        for kind in range(2):
            mine = kinds[kind][owner * owned : (owner + 1) * owned, :]
            out_ref[owner, kind] = mine


def add_hist(before, out_shape, bins, labels, elected, parts, shifts, n_feat, cores):
    features = bins.shape[0]
    classes, rows = parts[0].shape
    length = rows // 2
    count = len(parts)
    blocks = 2 * count
    group = min(features, 16)
    chained = before is not None
    final = out_shape is not None
    vmem = pl.BlockSpec(memory_space=pltpu.VMEM)
    far = pl.BlockSpec(memory_space=pltpu.HBM)
    near = pl.BlockSpec(memory_space=pl.ANY)
    sums = jax.ShapeDtypeStruct((features * BINS, 4 * classes), jnp.float32)
    out = jax.ShapeDtypeStruct(out_shape, jnp.float32) if final else None
    result = pl.pallas_call(
        lambda *refs: hist_kernel(group, length, shifts, n_feat, cores, chained, final, *refs),
        in_specs=[far, far, far] + [near] * count + [vmem] * chained,
        out_specs=[vmem, vmem] if final else [vmem],
        scratch_shapes=[
            pltpu.VMEM((2, features, length), jnp.int32),
            pltpu.VMEM((blocks, 1, length), jnp.int32),
            pltpu.VMEM((blocks, classes, length), jnp.bfloat16),
            pltpu.VMEM((4 * classes, length), F8),
            pltpu.VMEM((4 * classes, length), F8),
            pltpu.VMEM((4 * classes, 2 * classes), jnp.float32),
            pltpu.VMEM((4 * classes, 2 * classes), jnp.float32),
            pltpu.SemaphoreType.DMA((blocks,)),
            pltpu.SemaphoreType.DMA((blocks,)),
            pltpu.SemaphoreType.DMA((blocks,)),
            pltpu.VMEM(elected.shape, jnp.int32),
            pltpu.SemaphoreType.DMA,
            pltpu.VMEM((classes, 2 * classes), jnp.bfloat16),
        ],
        out_shape=[sums, out] if final else [sums],
        input_output_aliases={3 + count: 0} if chained else {},
        compiler_params=pltpu.CompilerParams(vmem_limit_bytes=36 << 20),
        cost_estimate=pl.CostEstimate(
            flops=2 * count * rows * features * BINS * 4 * classes,
            bytes_accessed=4 * count * rows * features,
            transcendentals=0,
        ),
    )(in_hbm(elected), in_hbm(bins), in_hbm(labels), *parts, *([before] if chained else []))
    return result[-1]


def gains_kernel(parts_ref, out_ref):
    hist = parts_ref[0]
    for part in range(1, parts_ref.shape[0]):
        hist = hist + parts_ref[part]
    _, owned, width = hist.shape
    hist = hist.reshape(2 * owned, width)
    lane = lax.broadcasted_iota(jnp.int32, hist.shape, 1) % BINS
    left = hist
    after = hist
    shift = 1
    while shift < BINS:
        left = left + jnp.where(lane >= shift, pltpu.roll(left, shift, 1), 0.0)
        after = after + jnp.where(lane < BINS - shift, pltpu.roll(after, width - shift, 1), 0.0)
        shift *= 2
    right = after - hist
    total = left + right
    left_g, left_h = left[:owned], left[owned:]
    right_g, right_h = right[:owned], right[owned:]
    tot_g, tot_h = total[:owned], total[owned:]
    gain = 0.5 * (
        left_g * left_g / (left_h + l2_penalty)
        + right_g * right_g / (right_h + l2_penalty)
        - tot_g * tot_g / (tot_h + l2_penalty)
    )
    for e in range(width // BINS):
        out_ref[:, e, :] = gain[:, e * BINS : (e + 1) * BINS - 1]


def shards(axis_sizes, scores, labels, bins, elected):
    n_rows, n_feat = axis_sizes
    own_rows, classes = scores.shape
    features = bins.shape[0]
    elect = elected.shape[1]
    owned = classes // n_rows
    labels = labels[None, :]
    cores = 2 if n_feat % 2 == 0 else 1
    chips = n_feat // cores
    swap = [(i, i ^ 1) for i in range(n_feat)]
    coded = score(scores.T, labels)

    def add(hist, parts, shifts, last):
        shape = (n_rows, 2, owned, elect * BINS) if last else None
        return add_hist(hist, shape, bins, labels, elected.T, parts, shifts, n_feat, cores)

    arrived = []
    for turn in range(1, chips):
        around = [(i, (i + turn * cores) % n_feat) for i in range(n_feat)]
        arrived.append(lax.ppermute(coded, "feat", around))
    if cores == 2:
        mate = lax.ppermute(coded, "feat", swap)
        hist = add(None, [coded, mate], [(0, 0), (0, 1)], chips == 1)
    else:
        hist = add(None, [coded], [(0, 0)], chips == 1)
    for turn, part in enumerate(arrived, 1):
        last = turn == chips - 1
        part, hist = lax.optimization_barrier((part, hist))
        mate = lax.ppermute(part, "feat", swap) if cores == 2 else None
        hist = add(hist, [part], [(turn, 0)], last and cores == 1)
        if cores == 2:
            hist = add(hist, [mate], [(turn, 1)], last)

    if n_rows > 1:
        hist = lax.all_to_all(hist, "rows", 0, 0, tiled=True)
    return pl.pallas_call(
        gains_kernel,
        out_shape=jax.ShapeDtypeStruct((owned, elect, BINS - 1), jnp.float32),
    )(hist)


def solution(mesh):
    sizes = (mesh.shape["rows"], mesh.shape["feat"])
    return jax.shard_map(
        lambda *arrays: shards(sizes, *arrays),
        mesh=mesh,
        in_specs=(P(("rows", "feat"), None), P("rows"), P("feat", "rows"), P(None, "feat")),
        out_specs=P("rows", "feat", None),
        check_vma=False,
    )
```

profile of v0, /device:TPU:0, one launch (start us, length us, event | category | flops | bytes accessed | tf_op | source)
XLA Modules:
  0.0 71.5 jit_solution(14720957868778524347)
XLA Ops:
  0.0 2.7 %shard_map.46.refs_3_ = bf16[64,8192]{1,0:T(8,128)(2,1)S(1)} custom-call(f32[64,8192]{1,0:T(8,128)} %bitcast.3, s32[1,32768]{1,0:T(1,128)} %bitcast.4), custom_call_target="tpu_custom_call" | custom-call | flops 5242880 | bytes 3145728 | tf_op jit(solution)/shard_map/pallas_call | solution.py:75
  2.7 0.5 collective-permute-start.1
  3.2 2.6 %collective-permute-start = (bf16[64,8192]{1,0:T(8,128)(2,1)S(1)}, bf16[64,8192]{1,0:T(8,128)(2,1)S(1)}, u32[]{:S(2)}, u32[]{:S(2)}) collective-permute-start(bf16[64,8192]{1,0:T(8,128)(2,1)S(1)} %shard_map.46.refs_3_), channel_id=1, source_target_pairs={{0,2},{1,3},{2,0},{3,1},{4,6},{5,7},{6,4},{7,5},{8,10},{9,11},{10,... | collective-permute-start | bytes 3145736 | tf_op jit(solution)/shard_map/ppermute | solution.py:394
  5.8 0.0 collective-permute-done.1.refs_4_
  5.8 23.5 %shard_map.47.refs_4_ = f32[4096,256]{1,0:T(8,128)S(1)} custom-call(s32[4,64]{1,0:T(4,128)} %bitcast.8, s32[64,32768]{1,0:T(8,128)} %refs_1_.5, s32[1,32768]{1,0:T(1,128)} %bitcast.5, bf16[64,8192]{1,0:T(8,128)(2,1)S(1)} %shard_map.46.refs_3_, bf16[64,8192]{1,0:T(8,128)(2,1)S(1)} %collective-permute-done.1.refs_4_), custom_call_target="tpu_custom_call" | custom-call | flops 34359738368 | bytes 4194304 | tf_op jit(solution)/shard_map/pallas_call | solution.py:316
  29.4 0.2 collective-permute-done.refs_3_
  29.6 0.0 collective-permute-start.2
  29.6 11.9 %shard_map.48.refs_4_ = f32[4096,256]{1,0:T(8,128)S(1)} custom-call(s32[4,64]{1,0:T(4,128)} %bitcast.9, s32[64,32768]{1,0:T(8,128)} %refs_1_.5, s32[1,32768]{1,0:T(1,128)} %bitcast.6, bf16[64,8192]{1,0:T(8,128)(2,1)S(1)} %collective-permute-done.refs_3_, f32[4096,256]{1,0:T(8,128)S(1)} %shard_map.47.refs_4_), custom_call_target="tpu_custom_call", output_to_operand_aliasing={{}: (4, {})} | custom-call | flops 17179869184 | bytes 2097152 | tf_op jit(solution)/shard_map/pallas_call | solution.py:316
  41.5 0.0 collective-permute-done.2.refs_3_
  41.5 13.7 %shard_map.49 = (f32[4096,256]{1,0:T(8,128)S(1)}, f32[8,2,8,256]{3,2,1,0:T(8,128)S(1)}) custom-call(s32[4,64]{1,0:T(4,128)} %bitcast.10, s32[64,32768]{1,0:T(8,128)} %refs_1_.5, s32[1,32768]{1,0:T(1,128)} %bitcast.7, bf16[64,8192]{1,0:T(8,128)(2,1)S(1)} %collective-permute-done.2.refs_3_, ...), custom_call_target="tpu_custom_call", output_to_operand_aliasing={{0}: (4, {})} | custom-call | flops 17179869184 | bytes 2097152 | tf_op jit(solution)/shard_map/pallas_call | solution.py:316
  55.3 14.3 %all_to_all.5.parts_ref = f32[8,2,8,256]{3,2,1,0:T(8,128)} all-to-all(f32[8,2,8,256]{3,2,1,0:T(8,128)S(1)} %get-tuple-element.10), channel_id=1, replica_groups=mesh['rows'=8,'feat'=4] {'rows'}, dimensions={0} | all-to-all | bytes 262144 | tf_op jit(solution)/shard_map/all_to_all | solution.py:409
  69.5 2.0 %shard_map.50 = f32[8,4,63]{2,1,0:T(4,128)} custom-call(f32[8,2,8,256]{3,2,1,0:T(8,128)} %all_to_all.5.parts_ref), custom_call_target="tpu_custom_call" | custom-call | tf_op jit(solution)/shard_map/pallas_call | solution.py:410
Async XLA Ops:
  2.7 3.1 %collective-permute-start.1 = (bf16[64,8192]{1,0:T(8,128)(2,1)S(1)}, bf16[64,8192]{1,0:T(8,128)(2,1)S(1)}, u32[]{:S(2)}, u32[]{:S(2)}) collective-permute-start(bf16[64,8192]{1,0:T(8,128)(2,1)S(1)} %shard_map.46.refs_3_), channel_id=1, source_target_pairs={{0,1},{1,0},{2,3},{3,2},{4,5},{5,4},{6,7},{7,6},{8,9},{9,8},{10,11... | collective-permute-start | bytes 3145736 | tf_op jit(solution)/shard_map/ppermute | solution.py:396
  3.2 26.3 %collective-permute-start = (bf16[64,8192]{1,0:T(8,128)(2,1)S(1)}, bf16[64,8192]{1,0:T(8,128)(2,1)S(1)}, u32[]{:S(2)}, u32[]{:S(2)}) collective-permute-start(bf16[64,8192]{1,0:T(8,128)(2,1)S(1)} %shard_map.46.refs_3_), channel_id=1, source_target_pairs={{0,2},{1,3},{2,0},{3,1},{4,6},{5,7},{6,4},{7,5},{8,10},{9,11},{10,... | collective-permute-start | bytes 3145736 | tf_op jit(solution)/shard_map/ppermute | solution.py:394
  29.6 11.9 %collective-permute-start.2 = (bf16[64,8192]{1,0:T(8,128)(2,1)S(1)}, bf16[64,8192]{1,0:T(8,128)(2,1)S(1)}, u32[]{:S(2)}, u32[]{:S(2)}) collective-permute-start(bf16[64,8192]{1,0:T(8,128)(2,1)S(1)} %collective-permute-done.refs_3_), channel_id=1, source_target_pairs={{0,1},{1,0},{2,3},{3,2},{4,5},{5,4},{6,7},{7,6},{8,9},{9,8},{10,11... | collective-permute-start | bytes 3145736 | tf_op jit(solution)/shard_map/ppermute | solution.py:403
where the time goes:
time: 71.8 us; the launch traced here: 71.5 us
  Pallas kernels  53.9 us (75%)
  blocking collectives  14.3 us (20%)
  starting transfers between devices  3.15 us (4%)
    pallas_call x3, Pallas kernels, add_hist(): pl.pallas_call(lambda *refs: hist_kernel(group, length, shifts, n_feat, c...  49.1 us
    all_to_all x1, blocking collectives, shards(): hist = lax.all_to_all(hist, 'rows', 0, 0, tiled=True)  14.3 us
    pallas_call x1, Pallas kernels, score(): pl.pallas_call(lambda *refs: score_kernel(n_blocks, *refs), in_specs=[far...  2.71 us
    ppermute x1, starting transfers between devices, shards(): arrived.append(lax.ppermute(coded, 'feat', around))  2.59 us
    pallas_call x1, Pallas kernels, shards(): pl.pallas_call(gains_kernel, out_shape=jax.ShapeDtypeStruct((owned, elect...  2.04 us
  transfers between devices with their start and end apart: 3, of which 1 were waited for; matrix products, arithmetic and copies ran while one was open for 0% of the time, Pallas kernels for 50%

commit v1 on v0

--- a/solution.py
+++ b/solution.py
@@ -70,7 +70,7 @@
 
 def score(scores, labels):
     classes, rows = scores.shape
-    n_blocks = 4
+    n_blocks = 8
     far = pl.BlockSpec(memory_space=pltpu.HBM)
     return pl.pallas_call(
         lambda *refs: score_kernel(n_blocks, *refs),
@@ -287,7 +287,7 @@
             return tuple(jnp.where(elected[e : e + 1, :] == feature, rows, picked[e]) for e in range(elect))
 
         nothing = tuple(jnp.zeros((BINS, width), jnp.float32) for _ in range(elect))
-        picked = lax.fori_loop(0, features, pick, nothing, unroll=2)
+        picked = lax.fori_loop(0, features, pick, nothing, unroll=8)
         by_class.append(jnp.concatenate([part.T for part in picked], axis=1))
     near = by_class[0][:classes] + by_class[0][classes:]
     square, whole = by_class[1][:classes], by_class[1][classes:]

time: 71.8 us -> 71.2 us (level)
  no operation moved by 1% of the time
where the time goes in v1:
time: 71.2 us; the launch traced here: 71 us
  Pallas kernels  53.3 us (75%)
  blocking collectives  14.3 us (20%)
  starting transfers between devices  3.15 us (4%)
    pallas_call x3, Pallas kernels, add_hist(): pl.pallas_call(lambda *refs: hist_kernel(group, length, shifts, n_feat, c...  48.6 us
    all_to_all x1, blocking collectives, shards(): hist = lax.all_to_all(hist, 'rows', 0, 0, tiled=True)  14.3 us
    pallas_call x1, Pallas kernels, score(): pl.pallas_call(lambda *refs: score_kernel(n_blocks, *refs), in_specs=[far...  2.68 us
    ppermute x1, starting transfers between devices, shards(): arrived.append(lax.ppermute(coded, 'feat', around))  2.59 us
    pallas_call x1, Pallas kernels, shards(): pl.pallas_call(gains_kernel, out_shape=jax.ShapeDtypeStruct((owned, elect...  2.04 us
  transfers between devices with their start and end apart: 3, of which 1 were waited for; matrix products, arithmetic and copies ran while one was open for 0% of the time, Pallas kernels for 50%

profile of v1, /device:TPU:0, one launch (start us, length us, event | category | flops | bytes accessed | tf_op | source)
XLA Modules:
  0.0 71.0 jit_solution(10408587408327256602)
XLA Ops:
  0.0 2.7 %shard_map.46.refs_3_ = bf16[64,8192]{1,0:T(8,128)(2,1)S(1)} custom-call(f32[64,8192]{1,0:T(8,128)} %bitcast.3, s32[1,32768]{1,0:T(1,128)} %bitcast.4), custom_call_target="tpu_custom_call" | custom-call | flops 5242880 | bytes 3145728 | tf_op jit(solution)/shard_map/pallas_call | solution.py:75
  2.7 0.5 collective-permute-start.1
  3.2 2.6 %collective-permute-start = (bf16[64,8192]{1,0:T(8,128)(2,1)S(1)}, bf16[64,8192]{1,0:T(8,128)(2,1)S(1)}, u32[]{:S(2)}, u32[]{:S(2)}) collective-permute-start(bf16[64,8192]{1,0:T(8,128)(2,1)S(1)} %shard_map.46.refs_3_), channel_id=1, source_target_pairs={{0,2},{1,3},{2,0},{3,1},{4,6},{5,7},{6,4},{7,5},{8,10},{9,11},{10,... | collective-permute-start | bytes 3145736 | tf_op jit(solution)/shard_map/ppermute | solution.py:394
  5.8 0.0 collective-permute-done.1.refs_4_
  5.8 23.5 %shard_map.47.refs_4_ = f32[4096,256]{1,0:T(8,128)S(1)} custom-call(s32[4,64]{1,0:T(4,128)} %bitcast.8, s32[64,32768]{1,0:T(8,128)} %refs_1_.5, s32[1,32768]{1,0:T(1,128)} %bitcast.5, bf16[64,8192]{1,0:T(8,128)(2,1)S(1)} %shard_map.46.refs_3_, bf16[64,8192]{1,0:T(8,128)(2,1)S(1)} %collective-permute-done.1.refs_4_), custom_call_target="tpu_custom_call" | custom-call | flops 34359738368 | bytes 4194304 | tf_op jit(solution)/shard_map/pallas_call | solution.py:316
  29.3 0.2 collective-permute-done.refs_3_
  29.5 0.0 collective-permute-start.2
  29.6 11.9 %shard_map.48.refs_4_ = f32[4096,256]{1,0:T(8,128)S(1)} custom-call(s32[4,64]{1,0:T(4,128)} %bitcast.9, s32[64,32768]{1,0:T(8,128)} %refs_1_.5, s32[1,32768]{1,0:T(1,128)} %bitcast.6, bf16[64,8192]{1,0:T(8,128)(2,1)S(1)} %collective-permute-done.refs_3_, f32[4096,256]{1,0:T(8,128)S(1)} %shard_map.47.refs_4_), custom_call_target="tpu_custom_call", output_to_operand_aliasing={{}: (4, {})} | custom-call | flops 17179869184 | bytes 2097152 | tf_op jit(solution)/shard_map/pallas_call | solution.py:316
  41.5 0.0 collective-permute-done.2.refs_3_
  41.5 13.2 %shard_map.49 = (f32[4096,256]{1,0:T(8,128)S(1)}, f32[8,2,8,256]{3,2,1,0:T(8,128)S(1)}) custom-call(s32[4,64]{1,0:T(4,128)} %bitcast.10, s32[64,32768]{1,0:T(8,128)} %refs_1_.5, s32[1,32768]{1,0:T(1,128)} %bitcast.7, bf16[64,8192]{1,0:T(8,128)(2,1)S(1)} %collective-permute-done.2.refs_3_, ...), custom_call_target="tpu_custom_call", output_to_operand_aliasing={{0}: (4, {})} | custom-call | flops 17179869184 | bytes 2097152 | tf_op jit(solution)/shard_map/pallas_call | solution.py:316
  54.7 14.3 %all_to_all.5.parts_ref = f32[8,2,8,256]{3,2,1,0:T(8,128)} all-to-all(f32[8,2,8,256]{3,2,1,0:T(8,128)S(1)} %get-tuple-element.10), channel_id=1, replica_groups=mesh['rows'=8,'feat'=4] {'rows'}, dimensions={0} | all-to-all | bytes 262144 | tf_op jit(solution)/shard_map/all_to_all | solution.py:409
  69.0 2.0 %shard_map.50 = f32[8,4,63]{2,1,0:T(4,128)} custom-call(f32[8,2,8,256]{3,2,1,0:T(8,128)} %all_to_all.5.parts_ref), custom_call_target="tpu_custom_call" | custom-call | tf_op jit(solution)/shard_map/pallas_call | solution.py:410
Async XLA Ops:
  2.7 3.1 %collective-permute-start.1 = (bf16[64,8192]{1,0:T(8,128)(2,1)S(1)}, bf16[64,8192]{1,0:T(8,128)(2,1)S(1)}, u32[]{:S(2)}, u32[]{:S(2)}) collective-permute-start(bf16[64,8192]{1,0:T(8,128)(2,1)S(1)} %shard_map.46.refs_3_), channel_id=1, source_target_pairs={{0,1},{1,0},{2,3},{3,2},{4,5},{5,4},{6,7},{7,6},{8,9},{9,8},{10,11... | collective-permute-start | bytes 3145736 | tf_op jit(solution)/shard_map/ppermute | solution.py:396
  3.2 26.3 %collective-permute-start = (bf16[64,8192]{1,0:T(8,128)(2,1)S(1)}, bf16[64,8192]{1,0:T(8,128)(2,1)S(1)}, u32[]{:S(2)}, u32[]{:S(2)}) collective-permute-start(bf16[64,8192]{1,0:T(8,128)(2,1)S(1)} %shard_map.46.refs_3_), channel_id=1, source_target_pairs={{0,2},{1,3},{2,0},{3,1},{4,6},{5,7},{6,4},{7,5},{8,10},{9,11},{10,... | collective-permute-start | bytes 3145736 | tf_op jit(solution)/shard_map/ppermute | solution.py:394
  29.5 11.9 %collective-permute-start.2 = (bf16[64,8192]{1,0:T(8,128)(2,1)S(1)}, bf16[64,8192]{1,0:T(8,128)(2,1)S(1)}, u32[]{:S(2)}, u32[]{:S(2)}) collective-permute-start(bf16[64,8192]{1,0:T(8,128)(2,1)S(1)} %collective-permute-done.refs_3_), channel_id=1, source_target_pairs={{0,1},{1,0},{2,3},{3,2},{4,5},{5,4},{6,7},{7,6},{8,9},{9,8},{10,11... | collective-permute-start | bytes 3145736 | tf_op jit(solution)/shard_map/ppermute | solution.py:403
